TPU v7x, 32 devices: a whole 2x2x4 slice. The times are simulated.
32 devices in a mesh: row: 8 (over y, x, core), col: 4 (over z).
Axes of the slice: x: 2, y: 2, z: 4, core: 2. Of those that a mesh axis runs over, the one named last changes fastest.
Arguments:
- amplitudes: bfloat16 [6144, 4096], P(('row', 'col')), may hold values from -4 to 4
- integrals: bfloat16 [4096, 4096], P('col', 'row'), may hold values from -0.25 to 0.25
- block_irrep: int32 [32], replicated, may hold values from 0 to 7
- occ_energy: float32 [6144], P('row'), may hold values from -6 to -2
- vir_energy: float32 [4096], P('col'), may hold values from 1 to 4
Outputs:
- new_amplitudes: float32 [6144, 4096], P('row', 'col')
All inputs are finite; a program needn't handle non-finite values.
Results may differ from a plain program's by a relative error of at most 0.0003.
Values may be sent and summed in bfloat16 or wider, within the bound.
A program may use at most 128 MiB of HBM per device.

v0:
```python
import jax
import jax.numpy as jnp
from jax import lax
from jax.sharding import PartitionSpec as P

VB = 128


def on_device(amplitudes, integrals, block_irrep, occ_energy, vir_energy):
    ab_local = integrals.shape[0]
    ab_start = lax.axis_index("col") * ab_local
    irrep = jnp.repeat(block_irrep, VB)
    row_irrep = lax.dynamic_slice_in_dim(irrep, ab_start, ab_local)
    whole_amps = lax.all_gather(amplitudes, "col", axis=0, tiled=True)
    piece = lax.all_gather(integrals, "row", axis=1, tiled=True)
    keep = row_irrep[:, None] == irrep[None, :]
    ladder = lax.dot_general(
        whole_amps,
        jnp.where(keep, piece, jnp.zeros_like(piece)),
        (((1,), (1,)), ((), ())),
        preferred_element_type=jnp.float32,
    )
    own = lax.dynamic_slice_in_dim(whole_amps, ab_start, ab_local, 1).astype(jnp.float32)
    return own + ladder / (occ_energy[:, None] - vir_energy[None, :])


def solution(mesh):
    return jax.shard_map(
        on_device,
        mesh=mesh,
        in_specs=(P(("row", "col"), None), P("col", "row"), P(), P("row"), P("col")),
        out_specs=P("row", "col"),
        check_vma=False,
    )
```

profile of v0, /device:TPU:1, one launch (start us, length us, event | category | flops | bytes accessed | tf_op | source)
XLA Modules:
  0.0 203.9 jit_solution(7786502567304802900)
XLA Ops:
  6.5 0.0 copy-start
  6.5 0.0 copy-start.1
  6.5 0.0 copy-start.2
  6.5 0.0 all-gather.3.cloned.1.call-start
  6.5 0.7 all-gather.3.cloned.1.call-update
  7.3 0.0 all-gather.5.cloned.1.call-start
  7.3 0.7 all-gather.5.cloned.1.call-update
  8.0 0.0 copy-done
  8.0 0.1 broadcast_bitcast_fusion
  8.1 118.5 %all-gather.3.cloned.1.call-done = bf16[768,4096]{1,0:T(8,128)(2,1)} async-done(((bf16[192,4096]{1,0:T(8,128)(2,1)}), bf16[768,4096]{1,0:T(8,128)(2,1)}) %all-gather.3.cloned.1.call-update) | async-done | bytes 6291472 | tf_op jit(solution)/shard_map/all_gather | solution.py:14
  126.6 1.5 constant_dynamic-slice_fusion
  128.2 1.6 copy.10
  129.7 53.2 %all-gather.5.cloned.1.call-done = bf16[1024,4096]{1,0:T(8,128)(2,1)} async-done(((bf16[1024,512]{1,0:T(8,128)(2,1)}), bf16[1024,4096]{1,0:T(8,128)(2,1)}) %all-gather.5.cloned.1.call-update) | async-done | bytes 8388624 | tf_op jit(solution)/shard_map/all_gather | solution.py:15
  182.9 0.0 copy-done.1
  182.9 0.0 copy-done.2
  182.9 11.7 %fusion.4 = f32[768,1024]{0,1:T(8,128)S(1)} fusion(bf16[768,1024]{0,1:T(8,128)(2,1)} %copy.10, bf16[768,4096]{1,0:T(8,128)(2,1)} %all-gather.3.cloned.1.call-done, bf16[1024,4096]{1,0:T(8,128)(2,1)} %all-gather.5.cloned.1.call-done, s32[4096]{0:T(1024)S(1)} %broadcast_bitcast_fusion, s32[1024]{0:T(1024)S(1)} %dynamic_slice.7, f32[1024]{0:T(1024)S(1)} %copy-done.1, ...), kind=kOutput, calls=%fused_computation.6 | convolution fusion | flops 6453985280 | bytes 19426304 | tf_op jit(solution)/shard_map/dot_general | solution.py:17
  194.7 2.4 %copy.9 = f32[768,1024]{1,0:T(8,128)} copy(f32[768,1024]{0,1:T(8,128)S(1)} %fusion.4) | data formatting | bytes 6291456 | tf_op jit(solution)/shard_map/add | solution.py:24
  (1 shorter events, 0.0 us)
Async XLA Ops:
  6.5 1.5 copy-start
  6.5 176.4 %copy-start.1 = (f32[1024]{0:T(1024)S(1)}, f32[1024]{0:T(1024)}, u32[]{:S(2)}) copy-start(f32[1024]{0:T(1024)} %param.9) | copy-start | bytes 12292
  6.5 176.4 %copy-start.2 = (f32[768]{0:T(1024)S(1)}, f32[768]{0:T(1024)}, u32[]{:S(2)}) copy-start(f32[768]{0:T(1024)} %param.8) | copy-start | bytes 9220
  6.5 120.1 %all-gather.3.cloned.1.call-start = ((), (), s32[]{:S(2)}) async-start(), calls=%async_computation | async-start | bytes 7864320 | tf_op jit(solution)/shard_map/all_gather | solution.py:14
  7.3 175.7 %all-gather.5.cloned.1.call-start = ((), (), s32[]{:S(2)}) async-start(), calls=%async_computation.1 | async-start | bytes 9437184 | tf_op jit(solution)/shard_map/all_gather | solution.py:15
Sparse Core Ops, SparseCore 0:
  8.9 117.6 all-gather.2
  128.5 54.3 all-gather.4
where the time goes:
time: 204 us
  waiting for transfers between devices  173 us (85%)
  between operations  13.4 us (7%)
  matrix products  11.7 us (6%)
  local copies, waits for them, and re-layouts  5.54 us (3%)
    all_gather x1, waiting for transfers between devices, on_device(): whole_amps = lax.all_gather(amplitudes, 'col', axis=0, tiled=True)  119 us
    all_gather x1, waiting for transfers between devices, on_device(): piece = lax.all_gather(integrals, 'row', axis=1, tiled=True)  53.2 us
    dot_general x1, matrix products, on_device(): lax.dot_general(whole_amps, jnp.where(keep, piece, jnp.zeros_like(piece))...  11.7 us
  transfers between devices with their start and end apart: 2, of which 2 were waited for; matrix products, arithmetic and copies ran while one was open for 2% of the time, Pallas kernels for 0%

commit v1 on v0

v1 whole, which is shorter than its diff:
```python
import functools

import jax
import jax.numpy as jnp
from jax import lax
from jax.experimental import pallas as pl
from jax.experimental.pallas import tpu as pltpu
from jax.sharding import PartitionSpec as P

VB = 128
MESH = pl.DeviceIdType.MESH


def by_collectives(amplitudes, integrals, block_irrep, occ_energy, vir_energy):
    ab_local = integrals.shape[0]
    ab_start = lax.axis_index("col") * ab_local
    irrep = jnp.repeat(block_irrep, VB)
    row_irrep = lax.dynamic_slice_in_dim(irrep, ab_start, ab_local)
    whole_amps = lax.all_gather(amplitudes, "col", axis=0, tiled=True)
    piece = lax.all_gather(integrals, "row", axis=1, tiled=True)
    keep = row_irrep[:, None] == irrep[None, :]
    ladder = lax.dot_general(
        whole_amps,
        jnp.where(keep, piece, jnp.zeros_like(piece)),
        (((1,), (1,)), ((), ())),
        preferred_element_type=jnp.float32,
    )
    own = lax.dynamic_slice_in_dim(whole_amps, ab_start, ab_local, 1).astype(jnp.float32)
    return own + ladder / (occ_energy[:, None] - vir_energy[None, :])


def kernel(ij, ab, cd, amps_hbm, itg_hbm, keep_ref, keep_far_ref, occ_ref, vir_ref, out_hbm,
           amp, itg, far, masked, acc, res, vir_far,
           load_a, load_i, store, up_s, up_r, dn_s, dn_r,
           i_s, i_r, f_s, f_r, j_s, j_r, v_s, v_r, res_s, res_r):
    r = lax.axis_index("row")
    z = lax.axis_index("col")
    core, x, y = r % 2, (r // 2) % 2, r // 4
    half = ab // 2
    inner = jnp.logical_and(z > 0, z < 3)

    def other(k):
        return ((y + k // 4) % 2) * 4 + ((x + (k // 2) % 2) % 2) * 2 + (core + k % 2) % 2

    barrier = pltpu.get_barrier_semaphore()
    for k in (1, 2, 4):
        pl.semaphore_signal(barrier, inc=1, device_id=(other(k), z), device_id_type=MESH)

    @pl.when(z < 3)
    def _():
        pl.semaphore_signal(barrier, inc=1, device_id=(r, z + 1), device_id_type=MESH)

    @pl.when(z > 0)
    def _():
        pl.semaphore_signal(barrier, inc=1, device_id=(r, z - 1), device_id_type=MESH)

    def load_amps(c):
        return pltpu.make_async_copy(amps_hbm.at[:, pl.ds(c * cd, cd)], amp.at[z, c], load_a.at[c])

    loads = [load_amps(c) for c in range(8)]
    load_itg = pltpu.make_async_copy(itg_hbm, itg.at[0], load_i)
    load_itg.start()
    for copy in loads:
        copy.start()
    load_itg.wait()
    for copy in loads:
        copy.wait()

    @pl.when(inner)
    def _():
        pl.semaphore_wait(barrier, 5)

    @pl.when(jnp.logical_not(inner))
    def _():
        pl.semaphore_wait(barrier, 4)

    def up(s, k):
        c = other(k)
        return pltpu.make_async_remote_copy(
            amp.at[z - s, c], amp.at[z - s, c], up_s.at[s, k], up_r.at[s, k],
            device_id=(r, z + 1), device_id_type=MESH)

    def up_in(s, k):
        c = other(k)
        return pltpu.make_async_remote_copy(
            amp.at[z - 1 - s, c], amp.at[z - 1 - s, c], up_s.at[s, k], up_r.at[s, k],
            device_id=(r, z - 1), device_id_type=MESH)

    def dn(s, k):
        c = other(k)
        return pltpu.make_async_remote_copy(
            amp.at[z + s, c], amp.at[z + s, c], dn_s.at[s, k], dn_r.at[s, k],
            device_id=(r, z - 1), device_id_type=MESH)

    def dn_in(s, k):
        c = other(k)
        return pltpu.make_async_remote_copy(
            amp.at[z + 1 + s, c], amp.at[z + 1 + s, c], dn_s.at[s, k], dn_r.at[s, k],
            device_id=(r, z + 1), device_id_type=MESH)

    def sends_up(s):
        return jnp.logical_and(z >= s, z < 2) if s == 0 else jnp.logical_and(z >= s, z < 3)

    def gets_up(s):
        return jnp.logical_and(z >= 1 + s, z < 3) if s == 0 else z >= 1 + s

    def sends_dn(s):
        return z >= 2 if s == 0 else jnp.logical_and(z > 0, z <= 3 - s)

    def gets_dn(s):
        return jnp.logical_and(z > 0, z <= 2) if s == 0 else z <= 2 - s

    def pass_on(s, k):
        @pl.when(gets_up(s))
        def _():
            up_in(s, k).wait_recv()
        if s < 2:
            @pl.when(sends_up(s + 1))
            def _():
                up(s + 1, k).start()

        @pl.when(gets_dn(s))
        def _():
            dn_in(s, k).wait_recv()
        if s < 2:
            @pl.when(sends_dn(s + 1))
            def _():
                dn(s + 1, k).start()

    def exchange(buf, send, recv):
        def part(k, h):
            return buf.at[k, pl.ds(h * half, half), :]

        def copy(k, h, to):
            return pltpu.make_async_remote_copy(
                part(k, h), part(k ^ to, h), send.at[to // 2, k, h], recv.at[k ^ to, h],
                device_id=(other(to), z), device_id_type=MESH)

        def arrived(k, h):
            pltpu.make_async_remote_copy(
                part(k, h), part(k, h), send.at[0, k, h], recv.at[k, h],
                device_id=(other(1), z), device_id_type=MESH).wait_recv()

        def first():
            for h in (0, 1):
                copy(0, h, 2).start()
                copy(0, h, 4).start()
                copy(0, h, 1).start()

        def second(h):
            arrived(2, h)
            arrived(4, h)
            if h == 0:
                copy(2, 0, 4).start()
            else:
                copy(4, 1, 2).start()
            copy(2, h, 1).start()
            copy(4, h, 1).start()

        def third():
            for h in (0, 1):
                arrived(6, h)
                copy(6, h, 1).start()

        def last():
            for h in (0, 1):
                for k in (1, 3, 5, 7):
                    arrived(k, h)

        def sent():
            for h in (0, 1):
                for to in (2, 4, 1):
                    copy(0, h, to).wait_send()
                for k in (2, 4, 6):
                    copy(k, h, 1).wait_send()
            copy(2, 0, 4).wait_send()
            copy(4, 1, 2).wait_send()

        return first, second, third, last, sent

    first, second, third, last, sent = exchange(itg, i_s, i_r)
    far_first, far_second, far_third, far_last, far_sent = exchange(far, f_s, f_r)

    inward = jnp.where(z == 0, 1, 2)

    def lend(h):
        return pltpu.make_async_remote_copy(
            itg.at[0, pl.ds(h * half, half), :], far.at[0, pl.ds(h * half, half), :],
            j_s.at[h], j_r.at[h], device_id=(r, inward), device_id_type=MESH)

    lend_vir = pltpu.make_async_remote_copy(
        vir_ref, vir_far, v_s, v_r, device_id=(r, inward), device_id_type=MESH)
    outward = jnp.where(z == 1, 0, 3)

    def give(h):
        s = pl.ds(h * (ij // 2), ij // 2)
        return pltpu.make_async_remote_copy(
            res.at[s, :], acc.at[z, s, :], res_s.at[h], res_r.at[h],
            device_id=(r, outward), device_id_type=MESH)

    @pl.when(jnp.logical_not(inner))
    def _():
        lend(0).start()
        lend(1).start()
        lend_vir.start()

    first()

    def own_out(k, carry):
        @pl.when(sends_up(0))
        def _():
            up(0, k).start()

        @pl.when(sends_dn(0))
        def _():
            dn(0, k).start()
        return carry

    lax.fori_loop(0, 8, own_out, 0)

    def has(q):
        away = jnp.where(q > z, q - z, z - q)
        near = jnp.where(inner, away >= 0, away != 1)
        return jnp.logical_and(near, away <= 2)

    def mask(buf, keep, k):
        c = other(k)
        for j in range(ab // VB):
            rows = pl.ds(j * VB, VB)
            m = keep[c, pl.ds(j, 1), :].astype(jnp.bfloat16)
            masked[k, rows, :] = buf[k, rows, :] * jnp.broadcast_to(m, (VB, cd))

    def term(q, k):
        return lax.dot_general(amp[q, other(k)], masked[k], (((1,), (1,)), ((), ())),
                               preferred_element_type=jnp.float32)

    def finish(q, target, total, vir, plane):
        for h in range(ab // cd):
            cols = pl.ds(h * cd, cd)
            own = amp[q, plane * (ab // cd) + h].astype(jnp.float32)
            target[:, cols] = own + total[:, cols] / (occ_ref[q] - vir[:, cols])

    def phase(s, lo, hi):
        def step(k, carry):
            pass_on(s, k)
            return carry
        lax.fori_loop(lo, hi, step, 0)

    phase(0, 0, 3)
    second(0)
    phase(0, 3, 6)
    second(1)
    phase(0, 6, 8)

    @pl.when(inner)
    def _():
        lend(0).wait_recv()
        lend(1).wait_recv()
        pltpu.make_async_remote_copy(
            vir_ref, vir_far, v_s, v_r, device_id=(r, inward), device_id_type=MESH).wait_recv()
        far_first()

    third()
    last()

    def multiply(k, carry):
        pass_on(1, k)
        mask(itg, keep_ref, k)

        def row_block(q, carry):
            @pl.when(has(q))
            def _():
                @pl.when(k == 0)
                def _():
                    acc[q] = term(q, k)

                @pl.when(k > 0)
                def _():
                    acc[q] += term(q, k)
            return carry

        lax.fori_loop(0, 4, row_block, 0)
        return carry

    lax.fori_loop(0, 3, multiply, 0)
    pl.when(inner)(lambda: far_second(0))
    lax.fori_loop(3, 6, multiply, 0)
    pl.when(inner)(lambda: far_second(1))
    lax.fori_loop(6, 8, multiply, 0)

    def put(q):
        return pltpu.make_async_copy(acc.at[q], out_hbm.at[pl.ds(q * ij, ij), :], store.at[q])

    def close(q, carry):
        @pl.when(has(q))
        def _():
            finish(q, acc.at[q], acc.at[q], vir_ref, z)
            put(q).start()
        return carry

    lax.fori_loop(0, 4, close, 0)

    @pl.when(inner)
    def _():
        far_third()

        def far_step(k, carry):
            mask(far, keep_far_ref, k)

            @pl.when(k == 0)
            def _():
                res[...] = term(z, k)

            @pl.when(k > 0)
            def _():
                res[...] += term(z, k)
            return carry

        far_last()
        lax.fori_loop(0, 8, far_step, 0)
        finish(z, res, res, vir_far, outward)
        give(0).start()
        give(1).start()
        far_sent()
        give(0).wait_send()
        give(1).wait_send()

    @pl.when(jnp.logical_not(inner))
    def _():
        q = 3 - z

        def step(k, carry):
            pass_on(2, k)

            @pl.when(k == 0)
            def _():
                acc[q] = term(q, k)

            @pl.when(k > 0)
            def _():
                acc[q] += term(q, k)
            return carry

        lax.fori_loop(0, 8, step, 0)
        finish(q, acc.at[q], acc.at[q], vir_ref, z)
        put(q).start()
        lend(0).wait_send()
        lend(1).wait_send()
        lend_vir.wait_send()
        for h in (0, 1):
            s = pl.ds(h * (ij // 2), ij // 2)
            pltpu.make_async_remote_copy(
                res.at[s, :], acc.at[inward, s, :], res_s.at[h], res_r.at[h],
                device_id=(r, inward), device_id_type=MESH).wait_recv()
        put(inward).start()

    sent()

    def drained(k, carry):
        for s in (0, 1, 2):
            @pl.when(sends_up(s))
            def _():
                up(s, k).wait_send()

            @pl.when(sends_dn(s))
            def _():
                dn(s, k).wait_send()
        return carry

    lax.fori_loop(0, 8, drained, 0)
    for q in range(4):
        put(q).wait()


def by_kernel(amplitudes, integrals, block_irrep, occ_energy, vir_energy):
    ij, all_cd = amplitudes.shape
    ab, cd = integrals.shape
    z = lax.axis_index("col")
    blocks = ab // VB
    columns = jnp.repeat(block_irrep, VB).reshape(8, 1, cd)

    def keep_of(plane):
        rows = lax.dynamic_slice_in_dim(block_irrep, plane * blocks, blocks)
        return (rows[None, :, None] == columns).astype(jnp.float32)

    vmem = pl.BlockSpec(memory_space=pltpu.VMEM)
    hbm = pl.BlockSpec(memory_space=pl.ANY)
    bf16, f32, dma = jnp.bfloat16, jnp.float32, pltpu.SemaphoreType.DMA
    return pl.pallas_call(
        functools.partial(kernel, ij, ab, cd),
        out_shape=jax.ShapeDtypeStruct((4 * ij, ab), f32),
        in_specs=[hbm, hbm, vmem, vmem, vmem, vmem],
        out_specs=hbm,
        scratch_shapes=[
            pltpu.VMEM((4, 8, ij, cd), bf16),
            pltpu.VMEM((8, ab, cd), bf16),
            pltpu.VMEM((8, ab, cd), bf16),
            pltpu.VMEM((8, ab, cd), bf16),
            pltpu.VMEM((4, ij, ab), f32),
            pltpu.VMEM((ij, ab), f32),
            pltpu.VMEM((1, ab), f32),
            dma((8,)), dma, dma((4,)),
            dma((3, 8)), dma((3, 8)), dma((3, 8)), dma((3, 8)),
            dma((3, 8, 2)), dma((8, 2)), dma((3, 8, 2)), dma((8, 2)),
            dma((2,)), dma((2,)), dma, dma, dma((2,)), dma((2,)),
        ],
        compiler_params=pltpu.CompilerParams(
            collective_id=0, has_side_effects=True, vmem_limit_bytes=56 * 2**20),
        cost_estimate=pl.CostEstimate(
            flops=10 * ij * ab * all_cd, bytes_accessed=8 * ij * ab * 4, transcendentals=0),
    )(amplitudes, integrals, keep_of(z), keep_of(3 * lax.shift_right_logical(z, 1)),
      occ_energy.reshape(4, ij, 1), vir_energy.reshape(1, ab))


def solution(mesh):
    line = mesh.shape["row"] == 8 and mesh.shape["col"] == 4
    return jax.shard_map(
        by_kernel if line else by_collectives,
        mesh=mesh,
        in_specs=(P(("row", "col"), None), P("col", "row"), P(), P("row"), P("col")),
        out_specs=P("row", "col"),
        check_vma=False,
    )
```

time: 204 us -> 136 us (0.67)
  waiting for transfers between devices: 173 us -> 0 us
  Pallas kernels: 0 us -> 127 us
  between operations: 13.4 us -> 0.01 us
  matrix products: 11.7 us -> 0 us
    all_gather x2 -> x0, waiting for transfers between devices: 172 us -> none  [the longest x1 119 us: on_device(): whole_amps = lax.all_gather(amplitudes, 'col', axis=0, tiled=True)]
    pallas_call x0 -> x1, Pallas kernels: none -> 127 us  [by_kernel(): pl.pallas_call(functools.partial(kernel, ij, ab, cd), out_shape=jax.Shape...]
    dot_general x1 -> x0, matrix products: 11.7 us -> none  [on_device(): lax.dot_general(whole_amps, jnp.where(keep, piece, jnp.zeros_like(piece))...]
    unnamed x7 -> x1, local copies, waits for them, and re-layouts: 1.58 us -> 3.97 us
    add x1 -> x0, local copies, waits for them, and re-layouts: 2.36 us -> none  [on_device(): return own + ladder / (occ_energy[:, None] - vir_energy[None, :])]
  transfers between devices with their start and end apart: 2 -> 0, of which waited for: 2 -> 0; matrix products, arithmetic and copies ran while one was open for 2% -> 0% of each run, Pallas kernels for 0% -> 0%
where the time goes in v1:
time: 136 us
  Pallas kernels  127 us (93%)
  local copies, waits for them, and re-layouts  7.36 us (5%)
    pallas_call x1, Pallas kernels, by_kernel(): pl.pallas_call(functools.partial(kernel, ij, ab, cd), out_shape=jax.Shape...  127 us
    unnamed x1, local copies, waits for them, and re-layouts  3.97 us

profile of v1, /device:TPU:1, one launch (start us, length us, event | category | flops | bytes accessed | tf_op | source)
XLA Modules:
  0.0 135.5 jit_solution(6801552115685854671)
XLA Ops:
  0.0 0.8 fusion
  0.8 0.7 broadcast_in_dim.9
  1.5 0.1 copy.7
  1.6 0.1 broadcast_bitcast_fusion
  1.7 0.8 compare_convert_fusion
  2.5 1.7 %reshape.16.occ_ref = f32[4,192,1]{2,1,0:T(8,128)} reshape(f32[768]{0:T(1024)} %param.8) | data formatting | bytes 6144 | tf_op jit(solution)/shard_map/reshape | solution.py:412
  4.2 127.3 %shard_map.55 = f32[768,1024]{1,0:T(8,128)} custom-call(bf16[192,4096]{1,0:T(8,128)(2,1)} %amps_hbm.1, bf16[1024,512]{1,0:T(8,128)(2,1)} %itg_hbm.1, f32[8,8,512]{2,1,0:T(8,128)} %get-tuple-element.6.keep_ref, f32[8,8,512]{2,1,0:T(8,128)} %get-tuple-element.5.keep_far_ref, f32[4,192,1]{2,1,0:T(8,128)} %reshape.16.occ_ref, f32[1,1024]{1,0:T(1,128)} %bitcast.3), custom_call_target="tpu_custom_call" | custom-call | flops 8053063680 | bytes 6291456 | tf_op jit(solution)/shard_map/pallas_call | solution.py:389
  131.5 4.0 %copy.10 = f32[768,1024]{1,0:T(8,128)} copy(f32[768,1024]{1,0:T(8,128)} %shard_map.55) | data formatting | bytes 6291456

commit v2 on v0

--- a/solution.py
+++ b/solution.py
@@ -1,12 +1,17 @@
+import functools
+
 import jax
 import jax.numpy as jnp
 from jax import lax
+from jax.experimental import pallas as pl
+from jax.experimental.pallas import tpu as pltpu
 from jax.sharding import PartitionSpec as P
 
 VB = 128
-
-
-def on_device(amplitudes, integrals, block_irrep, occ_energy, vir_energy):
+MESH = pl.DeviceIdType.MESH
+
+
+def by_collectives(amplitudes, integrals, block_irrep, occ_energy, vir_energy):
     ab_local = integrals.shape[0]
     ab_start = lax.axis_index("col") * ab_local
     irrep = jnp.repeat(block_irrep, VB)
@@ -24,9 +29,348 @@
     return own + ladder / (occ_energy[:, None] - vir_energy[None, :])
 
 
+def kernel(ij, ab, cd, amps_hbm, itg_hbm, irrep_ref, occ_ref, vir_ref, out_hbm,
+           amp, itg, far, masked, acc, res, vir_far, occ_rows,
+           load_a, load_i, store, up_s, up_r,
+           i_s, i_r, f_s, f_r, j_s, j_r, v_s, v_r, res_s, res_r):
+    r = lax.axis_index("row")
+    z = lax.axis_index("col")
+    core, x, y = r % 2, (r // 2) % 2, r // 4
+    half = ab // 2
+    inner = jnp.logical_and(z > 0, z < 3)
+
+    def other(k):
+        return ((y + k // 4) % 2) * 4 + ((x + (k // 2) % 2) % 2) * 2 + (core + k % 2) % 2
+
+    barrier = pltpu.get_barrier_semaphore()
+    for k in (1, 2, 4):
+        pl.semaphore_signal(barrier, inc=1, device_id=(other(k), z), device_id_type=MESH)
+
+    @pl.when(z < 3)
+    def _():
+        pl.semaphore_signal(barrier, inc=1, device_id=(r, z + 1), device_id_type=MESH)
+
+    @pl.when(z > 0)
+    def _():
+        pl.semaphore_signal(barrier, inc=1, device_id=(r, z - 1), device_id_type=MESH)
+
+    def load_amps(c):
+        return pltpu.make_async_copy(amps_hbm.at[:, pl.ds(c * cd, cd)], amp.at[z, c], load_a.at[c])
+
+    loads = [load_amps(c) for c in range(8)]
+    load_itg = pltpu.make_async_copy(itg_hbm, itg.at[0], load_i)
+    load_itg.start()
+    for copy in loads:
+        copy.start()
+    load_itg.wait()
+    for copy in loads:
+        copy.wait()
+
+    @pl.when(inner)
+    def _():
+        pl.semaphore_wait(barrier, 5)
+
+    @pl.when(jnp.logical_not(inner))
+    def _():
+        pl.semaphore_wait(barrier, 4)
+
+    def move(q, k, to, way):
+        c = other(k)
+        return pltpu.make_async_remote_copy(
+            amp.at[q, c], amp.at[q, c], up_s.at[way, q, k], up_r.at[q, k],
+            device_id=(r, to), device_id_type=MESH)
+
+    def exchange(buf, send, recv):
+        def part(k, h):
+            return buf.at[k, pl.ds(h * half, half), :]
+
+        def copy(k, h, to):
+            return pltpu.make_async_remote_copy(
+                part(k, h), part(k ^ to, h), send.at[to // 2, k, h], recv.at[k ^ to, h],
+                device_id=(other(to), z), device_id_type=MESH)
+
+        def arrived(k, h):
+            pltpu.make_async_remote_copy(
+                part(k, h), part(k, h), send.at[0, k, h], recv.at[k, h],
+                device_id=(other(1), z), device_id_type=MESH).wait_recv()
+
+        def first():
+            for h in (0, 1):
+                copy(0, h, 2).start()
+                copy(0, h, 4).start()
+                copy(0, h, 1).start()
+
+        def second(h):
+            arrived(2, h)
+            arrived(4, h)
+            if h == 0:
+                copy(2, 0, 4).start()
+            else:
+                copy(4, 1, 2).start()
+            copy(2, h, 1).start()
+            copy(4, h, 1).start()
+
+        def third():
+            for h in (0, 1):
+                arrived(6, h)
+                copy(6, h, 1).start()
+
+        def last(*which):
+            for h in (0, 1):
+                for k in which:
+                    arrived(k, h)
+
+        def sent():
+            for h in (0, 1):
+                for to in (2, 4, 1):
+                    copy(0, h, to).wait_send()
+                for k in (2, 4, 6):
+                    copy(k, h, 1).wait_send()
+            copy(2, 0, 4).wait_send()
+            copy(4, 1, 2).wait_send()
+
+        return first, second, third, last, sent
+
+    first, second, third, last, sent = exchange(itg, i_s, i_r)
+    far_first, far_second, far_third, far_last, far_sent = exchange(far, f_s, f_r)
+
+    inward = jnp.where(z == 0, 1, 2)
+    outward = jnp.where(z == 1, 0, 3)
+    peer = 3 - z
+
+    def lend(h):
+        return pltpu.make_async_remote_copy(
+            itg.at[0, pl.ds(h * half, half), :], far.at[0, pl.ds(h * half, half), :],
+            j_s.at[h], j_r.at[h], device_id=(r, inward), device_id_type=MESH)
+
+    lend_vir = pltpu.make_async_remote_copy(
+        vir_ref, vir_far, v_s, v_r, device_id=(r, inward), device_id_type=MESH)
+
+    def give(h, q, to):
+        s = pl.ds(h * (ij // 2), ij // 2)
+        return pltpu.make_async_remote_copy(
+            res.at[s, :], acc.at[q, s, :], res_s.at[h], res_r.at[h],
+            device_id=(r, to), device_id_type=MESH)
+
+    def loop(lo, hi, body):
+        def step(k, carry):
+            body(k)
+            return carry
+        lax.fori_loop(lo, hi, step, 0)
+
+    lane_block = lax.broadcasted_iota(jnp.int32, (1, cd), 1) // VB
+    per = cd // VB
+
+    def mask(buf, plane, k):
+        c = other(k)
+        columns = [irrep_ref[c * per + i] for i in range(per)]
+        for j in range(ab // VB):
+            line = irrep_ref[plane * (ab // VB) + j]
+            m = jnp.zeros((1, cd), jnp.float32)
+            for i in range(per):
+                same = jnp.where(columns[i] == line, 1.0, 0.0).astype(jnp.float32)
+                m = jnp.where(lane_block == i, same, m)
+            rows = pl.ds(j * VB, VB)
+            masked[k, rows, :] = buf[k, rows, :] * jnp.broadcast_to(m.astype(jnp.bfloat16), (VB, cd))
+
+    def term(q, k):
+        return lax.dot_general(amp[q, other(k)], masked[k], (((1,), (1,)), ((), ())),
+                               preferred_element_type=jnp.float32)
+
+    def add(q, k):
+        @pl.when(k == 0)
+        def _():
+            acc[q] = term(q, k)
+
+        @pl.when(k > 0)
+        def _():
+            acc[q] += term(q, k)
+
+    def far_add(*which):
+        for k in which:
+            mask(far, outward, k)
+            if k == 0:
+                res[...] = term(z, k)
+            else:
+                res[...] += term(z, k)
+
+    def finish(q, target, vir, plane):
+        rows = pl.ds(pl.multiple_of(q * ij, 8), ij)
+        for h in range(ab // cd):
+            cols = pl.ds(h * cd, cd)
+            own = amp[q, plane * (ab // cd) + h].astype(jnp.float32)
+            target[:, cols] = own + target[:, cols] / (occ_rows[rows, :1] - vir[:, cols])
+
+    def put(q):
+        return pltpu.make_async_copy(acc.at[q], out_hbm.at[pl.ds(q * ij, ij), :], store.at[q])
+
+    def close(q):
+        finish(q, acc.at[q], vir_ref, z)
+        put(q).start()
+
+    def flip():
+        occ_rows[...] = jnp.transpose(jnp.broadcast_to(occ_ref[...], (VB, 4 * ij)))
+
+    @pl.when(inner)
+    def _():
+        first()
+        loop(0, 8, lambda k: move(z, k, peer, 1).start())
+        flip()
+
+        def from_peer(k):
+            move(peer, k, peer, 0).wait_recv()
+            move(peer, k, outward, 0).start()
+
+        def from_end(k):
+            move(outward, k, outward, 1).wait_recv()
+            move(outward, k, peer, 1).start()
+
+        def from_far(k):
+            move(3 - outward, k, peer, 0).wait_recv()
+            move(3 - outward, k, outward, 0).start()
+
+        def both(k):
+            mask(itg, z, k)
+            add(z, k)
+            add(peer, k)
+
+        loop(0, 2, from_peer)
+        second(0)
+        loop(2, 5, from_peer)
+        second(1)
+        for h in (0, 1):
+            pltpu.make_async_remote_copy(
+                far.at[0, pl.ds(h * half, half), :], far.at[0, pl.ds(h * half, half), :],
+                j_s.at[h], j_r.at[h], device_id=(r, outward), device_id_type=MESH).wait_recv()
+        pltpu.make_async_remote_copy(
+            vir_ref, vir_far, v_s, v_r, device_id=(r, outward), device_id_type=MESH).wait_recv()
+        far_first()
+        loop(5, 8, lambda k: (from_peer(k), from_end(k - 5)))
+        third()
+        from_end(3)
+        from_far(0)
+        last(1, 3, 5, 7)
+        loop(0, 3, lambda k: (from_end(k + 4), from_far(k + 1), both(2 * k), both(2 * k + 1)))
+        far_second(0)
+        from_end(7)
+        from_far(4)
+        loop(6, 8, both)
+        far_second(1)
+        loop(0, 4, lambda k: add(outward, k))
+        from_far(5)
+        sent()
+        loop(4, 8, lambda k: add(outward, k))
+        close(z)
+        close(peer)
+        close(outward)
+        from_far(6)
+        far_add(0, 2, 4)
+        far_last(1, 3, 5)
+        far_add(1, 3, 5)
+        from_far(7)
+        far_third()
+        far_add(6)
+        far_last(7)
+        far_add(7)
+        finish(z, res, vir_far, outward)
+        give(0, z, outward).start()
+        give(1, z, outward).start()
+        loop(0, 8, lambda k: mask(itg, z, k))
+        loop(0, 8, lambda k: add(3 - outward, k))
+        close(3 - outward)
+        far_sent()
+
+        def drain(k):
+            move(z, k, peer, 1).wait_send()
+            move(peer, k, outward, 0).wait_send()
+            move(outward, k, peer, 1).wait_send()
+            move(3 - outward, k, outward, 0).wait_send()
+
+        loop(0, 8, drain)
+        give(0, z, outward).wait_send()
+        give(1, z, outward).wait_send()
+        for q in range(4):
+            put(q).wait()
+
+    @pl.when(jnp.logical_not(inner))
+    def _():
+        next_one = 3 - inward
+        lend(0).start()
+        lend(1).start()
+        lend_vir.start()
+        first()
+        flip()
+        second(0)
+        lend(0).wait_send()
+        loop(0, 2, lambda k: move(z, k, inward, 1).start())
+        lend(1).wait_send()
+        loop(2, 8, lambda k: move(z, k, inward, 1).start())
+        second(1)
+        third()
+        last(1, 3, 5, 7)
+
+        def near(k):
+            mask(itg, z, k)
+            add(z, k)
+            move(next_one, k, inward, 0).wait_recv()
+            add(next_one, k)
+
+        loop(0, 8, near)
+        close(z)
+        close(next_one)
+        sent()
+        lend_vir.wait_send()
+
+        def end(k):
+            move(peer, k, inward, 0).wait_recv()
+            add(peer, k)
+
+        loop(0, 8, end)
+        close(peer)
+        loop(0, 8, lambda k: move(z, k, inward, 1).wait_send())
+        give(0, inward, inward).wait_recv()
+        give(1, inward, inward).wait_recv()
+        put(inward).start()
+        for q in range(4):
+            put(q).wait()
+
+
+def by_kernel(amplitudes, integrals, block_irrep, occ_energy, vir_energy):
+    ij, all_cd = amplitudes.shape
+    ab, cd = integrals.shape
+    vmem = pl.BlockSpec(memory_space=pltpu.VMEM)
+    hbm = pl.BlockSpec(memory_space=pl.ANY)
+    bf16, f32, dma = jnp.bfloat16, jnp.float32, pltpu.SemaphoreType.DMA
+    return pl.pallas_call(
+        functools.partial(kernel, ij, ab, cd),
+        out_shape=jax.ShapeDtypeStruct((4 * ij, ab), f32),
+        in_specs=[hbm, hbm, pl.BlockSpec(memory_space=pltpu.SMEM), vmem, vmem],
+        out_specs=hbm,
+        scratch_shapes=[
+            pltpu.VMEM((4, 8, ij, cd), bf16),
+            pltpu.VMEM((8, ab, cd), bf16),
+            pltpu.VMEM((8, ab, cd), bf16),
+            pltpu.VMEM((8, ab, cd), bf16),
+            pltpu.VMEM((4, ij, ab), f32),
+            pltpu.VMEM((ij, ab), f32),
+            pltpu.VMEM((1, ab), f32),
+            pltpu.VMEM((4 * ij, VB), f32),
+            dma((8,)), dma, dma((4,)),
+            dma((2, 4, 8)), dma((4, 8)),
+            dma((3, 8, 2)), dma((8, 2)), dma((3, 8, 2)), dma((8, 2)),
+            dma((2,)), dma((2,)), dma, dma, dma((2,)), dma((2,)),
+        ],
+        compiler_params=pltpu.CompilerParams(
+            collective_id=0, has_side_effects=True, vmem_limit_bytes=40 * 2**20),
+        cost_estimate=pl.CostEstimate(
+            flops=10 * ij * ab * all_cd, bytes_accessed=8 * ij * ab * 4, transcendentals=0),
+    )(amplitudes, integrals, block_irrep, occ_energy.reshape(1, 4 * ij), vir_energy.reshape(1, ab))
+
+
 def solution(mesh):
+    line = mesh.shape["row"] == 8 and mesh.shape["col"] == 4
     return jax.shard_map(
-        on_device,
+        by_kernel if line else by_collectives,
         mesh=mesh,
         in_specs=(P(("row", "col"), None), P("col", "row"), P(), P("row"), P("col")),
         out_specs=P("row", "col"),

time: 204 us -> 105 us (0.51)
  waiting for transfers between devices: 173 us -> 0 us
  Pallas kernels: 0 us -> 98.3 us
  between operations: 13.4 us -> 0.01 us
  matrix products: 11.7 us -> 0 us
    all_gather x2 -> x0, waiting for transfers between devices: 172 us -> none  [the longest x1 119 us: on_device(): whole_amps = lax.all_gather(amplitudes, 'col', axis=0, tiled=True)]
    pallas_call x0 -> x1, Pallas kernels: none -> 98.3 us  [by_kernel(): pl.pallas_call(functools.partial(kernel, ij, ab, cd), out_shape=jax.Shape...]
    dot_general x1 -> x0, matrix products: 11.7 us -> none  [on_device(): lax.dot_general(whole_amps, jnp.where(keep, piece, jnp.zeros_like(piece))...]
    unnamed x7 -> x9, local copies, waits for them, and re-layouts: 1.58 us -> 5.64 us
    add x1 -> x0, local copies, waits for them, and re-layouts: 2.36 us -> none  [on_device(): return own + ladder / (occ_energy[:, None] - vir_energy[None, :])]
  transfers between devices with their start and end apart: 2 -> 0, of which waited for: 2 -> 0; matrix products, arithmetic and copies ran while one was open for 2% -> 0% of each run, Pallas kernels for 0% -> 0%
where the time goes in v2:
time: 105 us
  Pallas kernels  98.3 us (94%)
  local copies, waits for them, and re-layouts  6.33 us (6%)
    pallas_call x1, Pallas kernels, by_kernel(): pl.pallas_call(functools.partial(kernel, ij, ab, cd), out_shape=jax.Shape...  98.3 us
    unnamed x9, local copies, waits for them, and re-layouts  5.64 us

profile of v2, /device:TPU:1, one launch (start us, length us, event | category | flops | bytes accessed | tf_op | source)
XLA Modules:
  0.0 104.6 jit_solution(16769511311792640392)
XLA Ops:
  0.0 0.7 reshape.6.occ_ref
  0.7 0.0 copy-start
  0.7 1.4 %copy-done = bf16[192,4096]{1,0:T(8,128)(2,1)S(1)} copy-done((bf16[192,4096]{1,0:T(8,128)(2,1)S(1)}, bf16[192,4096]{1,0:T(8,128)(2,1)}, u32[]{:S(2)}) %copy-start) | copy-done | bytes 1572888
  2.1 0.0 copy-start.1
  2.1 1.2 %copy-done.1 = bf16[1024,512]{1,0:T(8,128)(2,1)S(1)} copy-done((bf16[1024,512]{1,0:T(8,128)(2,1)S(1)}, bf16[1024,512]{1,0:T(8,128)(2,1)}, u32[]{:S(2)}) %copy-start.1) | copy-done | bytes 1048600
  3.3 0.0 copy-start.2
  3.3 0.7 copy-done.2
  4.0 0.0 copy-start.3
  4.0 0.7 copy-done.3
  4.7 98.3 %shard_map.55 = f32[768,1024]{1,0:T(8,128)S(1)} custom-call(bf16[192,4096]{1,0:T(8,128)(2,1)S(1)} %copy-done, bf16[1024,512]{1,0:T(8,128)(2,1)S(1)} %copy-done.1, s32[32]{0:T(128)S(1)} %copy-done.3, f32[1,768]{1,0:T(1,128)S(1)} %reshape.6.occ_ref, f32[1,1024]{1,0:T(1,128)S(1)} %bitcast.1), custom_call_target="tpu_custom_call" | custom-call | flops 8053063680 | bytes 6291456 | tf_op jit(solution)/shard_map/pallas_call | solution.py:344
  102.9 1.7 %copy.7 = f32[768,1024]{1,0:T(8,128)} copy(f32[768,1024]{1,0:T(8,128)S(1)} %shard_map.55) | data formatting | bytes 6291456
Async XLA Ops:
  0.7 1.4 %copy-start = (bf16[192,4096]{1,0:T(8,128)(2,1)S(1)}, bf16[192,4096]{1,0:T(8,128)(2,1)}, u32[]{:S(2)}) copy-start(bf16[192,4096]{1,0:T(8,128)(2,1)} %amps_hbm.1) | copy-start | bytes 4718596
  2.1 1.2 %copy-start.1 = (bf16[1024,512]{1,0:T(8,128)(2,1)S(1)}, bf16[1024,512]{1,0:T(8,128)(2,1)}, u32[]{:S(2)}) copy-start(bf16[1024,512]{1,0:T(8,128)(2,1)} %itg_hbm.1) | copy-start | bytes 3145732
  3.3 0.7 copy-start.2
  4.0 0.7 copy-start.3

commit v3 on v2

--- a/solution.py
+++ b/solution.py
@@ -29,9 +29,9 @@
     return own + ladder / (occ_energy[:, None] - vir_energy[None, :])
 
 
-def kernel(ij, ab, cd, amps_hbm, itg_hbm, irrep_ref, occ_ref, vir_ref, out_hbm,
-           amp, itg, far, masked, acc, res, vir_far, occ_rows,
-           load_a, load_i, store, up_s, up_r,
+def kernel(ij, ab, cd, amps_hbm, itg_hbm, irrep_hbm, occ_ref, vir_ref, out_hbm,
+           irrep_ref, amp, itg, far, masked, masked_far, acc, res, vir_far, occ_rows,
+           load_a, load_i, load_b, store, up_s, up_r, e_s, e_r,
            i_s, i_r, f_s, f_r, j_s, j_r, v_s, v_r, res_s, res_r):
     r = lax.axis_index("row")
     z = lax.axis_index("col")
@@ -60,9 +60,12 @@
     loads = [load_amps(c) for c in range(8)]
     load_itg = pltpu.make_async_copy(itg_hbm, itg.at[0], load_i)
     load_itg.start()
+    load_irrep = pltpu.make_async_copy(irrep_hbm, irrep_ref, load_b)
+    load_irrep.start()
     for copy in loads:
         copy.start()
     load_itg.wait()
+    load_irrep.wait()
     for copy in loads:
         copy.wait()
 
@@ -80,6 +83,12 @@
             amp.at[q, c], amp.at[q, c], up_s.at[way, q, k], up_r.at[q, k],
             device_id=(r, to), device_id_type=MESH)
 
+    def carry_half(q, k, to, way):
+        part = amp.at[q, other(k % 8), pl.ds(pl.multiple_of((k // 8) * (ij // 2), 16), ij // 2), :]
+        return pltpu.make_async_remote_copy(
+            part, part, e_s.at[way, k], e_r.at[way, k],
+            device_id=(r, to), device_id_type=MESH)
+
     def exchange(buf, send, recv):
         def part(k, h):
             return buf.at[k, pl.ds(h * half, half), :]
@@ -94,11 +103,10 @@
                 part(k, h), part(k, h), send.at[0, k, h], recv.at[k, h],
                 device_id=(other(1), z), device_id_type=MESH).wait_recv()
 
-        def first():
-            for h in (0, 1):
-                copy(0, h, 2).start()
-                copy(0, h, 4).start()
-                copy(0, h, 1).start()
+        def first(h):
+            copy(0, h, 2).start()
+            copy(0, h, 4).start()
+            copy(0, h, 1).start()
 
         def second(h):
             arrived(2, h)
@@ -146,10 +154,10 @@
     lend_vir = pltpu.make_async_remote_copy(
         vir_ref, vir_far, v_s, v_r, device_id=(r, inward), device_id_type=MESH)
 
-    def give(h, q, to):
-        s = pl.ds(h * (ij // 2), ij // 2)
+    def give(n, q, to):
+        s = pl.ds((n % 2) * (ij // 2), ij // 2)
         return pltpu.make_async_remote_copy(
-            res.at[s, :], acc.at[q, s, :], res_s.at[h], res_r.at[h],
+            res.at[n // 2, s, :], acc.at[q, s, :], res_s.at[n], res_r.at[n],
             device_id=(r, to), device_id_type=MESH)
 
     def loop(lo, hi, body):
@@ -161,7 +169,7 @@
     lane_block = lax.broadcasted_iota(jnp.int32, (1, cd), 1) // VB
     per = cd // VB
 
-    def mask(buf, plane, k):
+    def mask(buf, out, plane, k):
         c = other(k)
         columns = [irrep_ref[c * per + i] for i in range(per)]
         for j in range(ab // VB):
@@ -171,7 +179,7 @@
                 same = jnp.where(columns[i] == line, 1.0, 0.0).astype(jnp.float32)
                 m = jnp.where(lane_block == i, same, m)
             rows = pl.ds(j * VB, VB)
-            masked[k, rows, :] = buf[k, rows, :] * jnp.broadcast_to(m.astype(jnp.bfloat16), (VB, cd))
+            out[k, rows, :] = buf[k, rows, :] * jnp.broadcast_to(m.astype(jnp.bfloat16), (VB, cd))
 
     def term(q, k):
         return lax.dot_general(amp[q, other(k)], masked[k], (((1,), (1,)), ((), ())),
@@ -188,18 +196,34 @@
 
     def far_add(*which):
         for k in which:
-            mask(far, outward, k)
+            mask(far, masked_far, outward, k)
+            t = lax.dot_general(amp[z, other(k)], masked_far[k], (((1,), (1,)), ((), ())),
+                                preferred_element_type=jnp.float32)
             if k == 0:
-                res[...] = term(z, k)
+                res[0] = t
             else:
-                res[...] += term(z, k)
-
-    def finish(q, target, vir, plane):
-        rows = pl.ds(pl.multiple_of(q * ij, 8), ij)
+                res[0] += t
+
+    def far_half(h, k):
+        rows = pl.ds(h * (ij // 2), ij // 2)
+        t = lax.dot_general(amp[3 - outward, other(k), rows, :], masked_far[k],
+                            (((1,), (1,)), ((), ())), preferred_element_type=jnp.float32)
+
+        @pl.when(k == 0)
+        def _():
+            res[1, rows, :] = t
+
+        @pl.when(k > 0)
+        def _():
+            res[1, rows, :] += t
+
+    def finish(q, target, vir, plane, first_row=0, n_rows=ij):
+        rows = pl.ds(pl.multiple_of(q * ij + first_row, 8), n_rows)
+        here = pl.ds(first_row, n_rows)
         for h in range(ab // cd):
             cols = pl.ds(h * cd, cd)
-            own = amp[q, plane * (ab // cd) + h].astype(jnp.float32)
-            target[:, cols] = own + target[:, cols] / (occ_rows[rows, :1] - vir[:, cols])
+            own = amp[q, plane * (ab // cd) + h, here, :].astype(jnp.float32)
+            target[here, cols] = own + target[here, cols] / (occ_rows[rows, :1] - vir[:, cols])
 
     def put(q):
         return pltpu.make_async_copy(acc.at[q], out_hbm.at[pl.ds(q * ij, ij), :], store.at[q])
@@ -213,7 +237,6 @@
 
     @pl.when(inner)
     def _():
-        first()
         loop(0, 8, lambda k: move(z, k, peer, 1).start())
         flip()
 
@@ -222,73 +245,75 @@
             move(peer, k, outward, 0).start()
 
         def from_end(k):
-            move(outward, k, outward, 1).wait_recv()
-            move(outward, k, peer, 1).start()
+            carry_half(outward, k, outward, 0).wait_recv()
+            carry_half(outward, k, peer, 1).start()
 
         def from_far(k):
-            move(3 - outward, k, peer, 0).wait_recv()
-            move(3 - outward, k, outward, 0).start()
-
-        def both(k):
-            mask(itg, z, k)
+            carry_half(3 - outward, k, peer, 1).wait_recv()
+
+        def half_of_far(h):
+            loop(0, 8, lambda k: (from_far(h * 8 + k), far_half(h, k)))
+            finish(3 - outward, res.at[1], vir_far, outward, h * (ij // 2), ij // 2)
+            give(2 + h, 3 - outward, outward).start()
+
+        def near(k):
+            mask(itg, masked, z, k)
             add(z, k)
             add(peer, k)
 
-        loop(0, 2, from_peer)
-        second(0)
-        loop(2, 5, from_peer)
-        second(1)
+        loop(0, 3, from_peer)
         for h in (0, 1):
             pltpu.make_async_remote_copy(
                 far.at[0, pl.ds(h * half, half), :], far.at[0, pl.ds(h * half, half), :],
                 j_s.at[h], j_r.at[h], device_id=(r, outward), device_id_type=MESH).wait_recv()
+            far_first(h)
+            loop(3 + 2 * h, 5 + 2 * h, from_peer)
         pltpu.make_async_remote_copy(
             vir_ref, vir_far, v_s, v_r, device_id=(r, outward), device_id_type=MESH).wait_recv()
-        far_first()
-        loop(5, 8, lambda k: (from_peer(k), from_end(k - 5)))
-        third()
-        from_end(3)
-        from_far(0)
-        last(1, 3, 5, 7)
-        loop(0, 3, lambda k: (from_end(k + 4), from_far(k + 1), both(2 * k), both(2 * k + 1)))
         far_second(0)
-        from_end(7)
-        from_far(4)
-        loop(6, 8, both)
+        loop(0, 3, from_end)
+        from_peer(7)
         far_second(1)
-        loop(0, 4, lambda k: add(outward, k))
-        from_far(5)
-        sent()
-        loop(4, 8, lambda k: add(outward, k))
-        close(z)
-        close(peer)
-        close(outward)
-        from_far(6)
+        first(0)
+        first(1)
+        loop(3, 6, from_end)
         far_add(0, 2, 4)
         far_last(1, 3, 5)
         far_add(1, 3, 5)
-        from_far(7)
         far_third()
         far_add(6)
         far_last(7)
         far_add(7)
-        finish(z, res, vir_far, outward)
+        finish(z, res.at[0], vir_far, outward)
         give(0, z, outward).start()
         give(1, z, outward).start()
-        loop(0, 8, lambda k: mask(itg, z, k))
-        loop(0, 8, lambda k: add(3 - outward, k))
+        loop(6, 9, from_end)
+        second(0)
+        loop(9, 12, from_end)
+        half_of_far(0)
+        second(1)
+        loop(12, 16, from_end)
+        third()
+        half_of_far(1)
+        last(1, 3, 5, 7)
+        loop(0, 8, near)
+        close(z)
+        close(peer)
+        loop(0, 8, lambda k: (add(outward, k), add(3 - outward, k)))
+        close(outward)
         close(3 - outward)
+        sent()
         far_sent()
 
         def drain(k):
             move(z, k, peer, 1).wait_send()
             move(peer, k, outward, 0).wait_send()
-            move(outward, k, peer, 1).wait_send()
-            move(3 - outward, k, outward, 0).wait_send()
+            carry_half(outward, k, peer, 1).wait_send()
+            carry_half(outward, k + 8, peer, 1).wait_send()
 
         loop(0, 8, drain)
-        give(0, z, outward).wait_send()
-        give(1, z, outward).wait_send()
+        for n in range(4):
+            give(n, z, outward).wait_send()
         for q in range(4):
             put(q).wait()
 
@@ -298,19 +323,20 @@
         lend(0).start()
         lend(1).start()
         lend_vir.start()
-        first()
+        first(0)
+        first(1)
         flip()
         second(0)
         lend(0).wait_send()
-        loop(0, 2, lambda k: move(z, k, inward, 1).start())
+        loop(0, 3, lambda k: carry_half(z, k, inward, 0).start())
         lend(1).wait_send()
-        loop(2, 8, lambda k: move(z, k, inward, 1).start())
+        loop(3, 16, lambda k: carry_half(z, k, inward, 0).start())
         second(1)
         third()
         last(1, 3, 5, 7)
 
         def near(k):
-            mask(itg, z, k)
+            mask(itg, masked, z, k)
             add(z, k)
             move(next_one, k, inward, 0).wait_recv()
             add(next_one, k)
@@ -321,16 +347,13 @@
         sent()
         lend_vir.wait_send()
 
-        def end(k):
-            move(peer, k, inward, 0).wait_recv()
-            add(peer, k)
-
-        loop(0, 8, end)
-        close(peer)
-        loop(0, 8, lambda k: move(z, k, inward, 1).wait_send())
+        loop(0, 16, lambda k: carry_half(z, k, inward, 0).wait_send())
         give(0, inward, inward).wait_recv()
         give(1, inward, inward).wait_recv()
         put(inward).start()
+        give(2, peer, inward).wait_recv()
+        give(3, peer, inward).wait_recv()
+        put(peer).start()
         for q in range(4):
             put(q).wait()
 
@@ -339,29 +362,31 @@
     ij, all_cd = amplitudes.shape
     ab, cd = integrals.shape
     vmem = pl.BlockSpec(memory_space=pltpu.VMEM)
-    hbm = pl.BlockSpec(memory_space=pl.ANY)
+    hbm = pl.BlockSpec(memory_space=pltpu.HBM)
     bf16, f32, dma = jnp.bfloat16, jnp.float32, pltpu.SemaphoreType.DMA
     return pl.pallas_call(
         functools.partial(kernel, ij, ab, cd),
         out_shape=jax.ShapeDtypeStruct((4 * ij, ab), f32),
-        in_specs=[hbm, hbm, pl.BlockSpec(memory_space=pltpu.SMEM), vmem, vmem],
-        out_specs=hbm,
+        in_specs=[hbm, hbm, hbm, vmem, vmem],
+        out_specs=pl.BlockSpec(memory_space=pl.ANY),
         scratch_shapes=[
+            pltpu.SMEM((all_cd // VB,), jnp.int32),
             pltpu.VMEM((4, 8, ij, cd), bf16),
             pltpu.VMEM((8, ab, cd), bf16),
             pltpu.VMEM((8, ab, cd), bf16),
             pltpu.VMEM((8, ab, cd), bf16),
+            pltpu.VMEM((8, ab, cd), bf16),
             pltpu.VMEM((4, ij, ab), f32),
-            pltpu.VMEM((ij, ab), f32),
+            pltpu.VMEM((2, ij, ab), f32),
             pltpu.VMEM((1, ab), f32),
             pltpu.VMEM((4 * ij, VB), f32),
-            dma((8,)), dma, dma((4,)),
-            dma((2, 4, 8)), dma((4, 8)),
+            dma((8,)), dma, dma, dma((4,)),
+            dma((2, 4, 8)), dma((4, 8)), dma((2, 16)), dma((2, 16)),
             dma((3, 8, 2)), dma((8, 2)), dma((3, 8, 2)), dma((8, 2)),
-            dma((2,)), dma((2,)), dma, dma, dma((2,)), dma((2,)),
+            dma((2,)), dma((2,)), dma, dma, dma((4,)), dma((4,)),
         ],
         compiler_params=pltpu.CompilerParams(
-            collective_id=0, has_side_effects=True, vmem_limit_bytes=40 * 2**20),
+            collective_id=0, has_side_effects=True, vmem_limit_bytes=48 * 2**20),
         cost_estimate=pl.CostEstimate(
             flops=10 * ij * ab * all_cd, bytes_accessed=8 * ij * ab * 4, transcendentals=0),
     )(amplitudes, integrals, block_irrep, occ_energy.reshape(1, 4 * ij), vir_energy.reshape(1, ab))

time: 105 us -> 116 us (1.10)
  the two profiles are of different devices: /device:TPU:1 before, /device:TPU:8 now
where the time goes in v3:
time: 116 us
  Pallas kernels  110 us (95%)
  local copies, waits for them, and re-layouts  6.33 us (5%)
    pallas_call x1, Pallas kernels, by_kernel(): pl.pallas_call(functools.partial(kernel, ij, ab, cd), out_shape=jax.Shape...  110 us
    unnamed x9, local copies, waits for them, and re-layouts  5.64 us

profile of v3, /device:TPU:8, one launch (start us, length us, event | category | flops | bytes accessed | tf_op | source)
XLA Modules:
  0.0 116.2 jit_solution(1057571678197718477)
XLA Ops:
  0.0 0.7 reshape.6.occ_ref
  0.7 0.0 copy-start
  0.7 1.4 %copy-done = bf16[192,4096]{1,0:T(8,128)(2,1)S(1)} copy-done((bf16[192,4096]{1,0:T(8,128)(2,1)S(1)}, bf16[192,4096]{1,0:T(8,128)(2,1)}, u32[]{:S(2)}) %copy-start) | copy-done | bytes 1572888
  2.1 0.0 copy-start.1
  2.1 1.2 %copy-done.1 = bf16[1024,512]{1,0:T(8,128)(2,1)S(1)} copy-done((bf16[1024,512]{1,0:T(8,128)(2,1)S(1)}, bf16[1024,512]{1,0:T(8,128)(2,1)}, u32[]{:S(2)}) %copy-start.1) | copy-done | bytes 1048600
  3.3 0.0 copy-start.2
  3.3 0.7 copy-done.2
  4.0 0.0 copy-start.3
  4.0 0.7 copy-done.3
  4.7 109.9 %shard_map.55 = f32[768,1024]{1,0:T(8,128)S(1)} custom-call(bf16[192,4096]{1,0:T(8,128)(2,1)S(1)} %copy-done, bf16[1024,512]{1,0:T(8,128)(2,1)S(1)} %copy-done.1, s32[32]{0:T(128)S(1)} %copy-done.3, f32[1,768]{1,0:T(1,128)S(1)} %reshape.6.occ_ref, f32[1,1024]{1,0:T(1,128)S(1)} %bitcast.1), custom_call_target="tpu_custom_call" | custom-call | flops 8053063680 | bytes 6291456 | tf_op jit(solution)/shard_map/pallas_call | solution.py:367
  114.6 1.7 %copy.7 = f32[768,1024]{1,0:T(8,128)} copy(f32[768,1024]{1,0:T(8,128)S(1)} %shard_map.55) | data formatting | bytes 6291456
Async XLA Ops:
  0.7 1.4 %copy-start = (bf16[192,4096]{1,0:T(8,128)(2,1)S(1)}, bf16[192,4096]{1,0:T(8,128)(2,1)}, u32[]{:S(2)}) copy-start(bf16[192,4096]{1,0:T(8,128)(2,1)} %amps_hbm.1) | copy-start | bytes 4718596
  2.1 1.2 %copy-start.1 = (bf16[1024,512]{1,0:T(8,128)(2,1)S(1)}, bf16[1024,512]{1,0:T(8,128)(2,1)}, u32[]{:S(2)}) copy-start(bf16[1024,512]{1,0:T(8,128)(2,1)} %itg_hbm.1) | copy-start | bytes 3145732
  3.3 0.7 copy-start.2
  4.0 0.7 copy-start.3
